TPU v7x, 32 devices: a whole 2x2x4 slice. The times are simulated.
32 devices in a mesh: seq: 8 (over z, y), head: 4 (over x, core).
Axes of the slice: x: 2, y: 2, z: 4, core: 2. Of those that a mesh axis runs over, the one named last changes fastest.
Arguments:
- queries: bfloat16 [1024, 8, 1024], P('seq', 'head'), may hold values from -6 to 6
- keys: bfloat16 [1024, 1024], P('seq', 'head'), may hold values from -6 to 6
- values: bfloat16 [1024, 1024], P('seq', 'head'), may hold values from -6 to 6
- out_grad: bfloat16 [1024, 8, 1024], P('seq', 'head'), may hold values from -6 to 6
- doc_ids: int32 [1024], P('seq'), may hold values from 0 to 3, never falling along the last dimension, each value on 1 to 384 neighbouring positions
Outputs:
- attended: bfloat16 [1024, 8, 1024], P('seq', 'head')
- query_grad: bfloat16 [1024, 8, 1024], P('seq', 'head')
- key_grad: bfloat16 [1024, 1024], P('seq', 'head')
- value_grad: bfloat16 [1024, 1024], P('seq', 'head')
Inputs may be any that keep to these rules, and one draw needn't show every extreme that they name: `doc_ids`: document ids never fall; each document has at most 384 tokens, one exactly that many.
All inputs are finite; a program needn't handle non-finite values.
Results may differ from a plain program's by a relative error of at most 0.0067.
Values may be sent and summed in bfloat16 or wider, within the bound.
A program may use at most 64 MiB of HBM per device.

v0:
```python
import math

import jax
import jax.numpy as jnp
from jax import lax
from jax.sharding import PartitionSpec as P

HD = 128
REACH = 3


def passed_along(value, axis, steps):
    count = lax.axis_size(axis)
    leading, last = (max(0, -steps), min(count, count - steps))
    return lax.ppermute(value, axis, [(source, source + steps) for source in range(leading, last)])


def attend(query_blk, grad_blk, key_win, value_win, seg_rows, seg_keys):
    rows_n = query_blk.shape[0]
    width = key_win.shape[0]
    scale = 1.0 / math.sqrt(HD)
    row_pos = lax.broadcasted_iota(jnp.int32, (rows_n, width), 0) + (width - rows_n)
    col_pos = lax.broadcasted_iota(jnp.int32, (rows_n, width), 1)
    allowed = (seg_rows[:, None] == seg_keys[None, :]) & (col_pos <= row_pos)
    scores = (
        jnp.einsum("trgd,ugd->grtu", query_blk, key_win, preferred_element_type=jnp.float32) * scale
    )
    scores = jnp.where(allowed, scores, -1e30)
    row_max = jnp.max(scores, axis=-1, keepdims=True)
    expo = jnp.where(allowed, jnp.exp(scores - row_max), 0.0)
    probs = expo / jnp.sum(expo, axis=-1, keepdims=True)
    probs_b = probs.astype(jnp.bfloat16)
    attended = jnp.einsum(
        "grtu,ugd->trgd", probs_b, value_win, preferred_element_type=jnp.float32
    ).astype(jnp.bfloat16)
    dprob = jnp.einsum("trgd,ugd->grtu", grad_blk, value_win, preferred_element_type=jnp.float32)
    delta = jnp.sum(probs * dprob, axis=-1, keepdims=True)
    dscore = (probs * (dprob - delta) * scale).astype(jnp.bfloat16)
    query_grad = jnp.einsum(
        "grtu,ugd->trgd", dscore, key_win, preferred_element_type=jnp.float32
    ).astype(jnp.bfloat16)
    key_grad = jnp.einsum("grtu,trgd->ugd", dscore, query_blk, preferred_element_type=jnp.float32)
    value_grad = jnp.einsum("grtu,trgd->ugd", probs_b, grad_blk, preferred_element_type=jnp.float32)
    return (attended, query_grad, key_grad, value_grad)


def on_device(queries, keys, values, out_grad, doc_ids):
    rows_n = queries.shape[0]
    reps_here = queries.shape[1]
    groups_total = queries.shape[2] // HD
    width = (REACH + 1) * rows_n
    marks = doc_ids + 1
    wide_keys, wide_values = (
        lax.all_gather(keys, "head", axis=1, tiled=True),
        lax.all_gather(values, "head", axis=1, tiled=True),
    )
    key_list = []
    value_list = []
    seg_list = []
    for step in range(REACH, 0, -1):
        prev_keys, prev_values, prev_marks = passed_along(
            (wide_keys, wide_values, marks), "seq", step
        )
        key_list.append(prev_keys)
        value_list.append(prev_values)
        seg_list.append(prev_marks - 1)
    key_win = jnp.concatenate(key_list + [wide_keys], axis=0).reshape(width, groups_total, HD)
    value_win = jnp.concatenate(value_list + [wide_values], axis=0).reshape(width, groups_total, HD)
    seg_keys = jnp.concatenate(seg_list + [doc_ids], axis=0)
    attended, query_grad, key_grad, value_grad = attend(
        queries.reshape(rows_n, reps_here, groups_total, HD),
        out_grad.reshape(rows_n, reps_here, groups_total, HD),
        key_win,
        value_win,
        doc_ids,
        seg_keys,
    )
    total_keys = key_grad[REACH * rows_n :]
    total_values = value_grad[REACH * rows_n :]
    for step in range(1, REACH + 1):
        lower = (REACH - step) * rows_n
        back_keys, back_values = passed_along(
            (key_grad[lower : lower + rows_n], value_grad[lower : lower + rows_n]), "seq", -step
        )
        total_keys = total_keys + back_keys
        total_values = total_values + back_values
    summed_keys, summed_values = (
        lax.psum_scatter(
            total_keys.reshape(rows_n, groups_total * HD), "head", scatter_dimension=1, tiled=True
        ),
        lax.psum_scatter(
            total_values.reshape(rows_n, groups_total * HD), "head", scatter_dimension=1, tiled=True
        ),
    )
    key_out = summed_keys.astype(jnp.bfloat16)
    value_out = summed_values.astype(jnp.bfloat16)
    attended_out = attended.reshape(rows_n, reps_here, groups_total * HD)
    query_out = query_grad.reshape(rows_n, reps_here, groups_total * HD)
    return (attended_out, query_out, key_out, value_out)


def solution(mesh):
    in_specs = (
        P("seq", "head", None),
        P("seq", "head"),
        P("seq", "head"),
        P("seq", "head", None),
        P("seq"),
    )
    out_specs = (P("seq", "head", None), P("seq", "head", None), P("seq", "head"), P("seq", "head"))
    return jax.shard_map(
        on_device, mesh=mesh, in_specs=in_specs, out_specs=out_specs, check_vma=False
    )
```

profile of v0, /device:TPU:1, one launch (start us, length us, event | category | flops | bytes accessed | tf_op | source)
XLA Modules:
  0.0 218.1 jit_solution(11056721715754741147)
XLA Ops:
  7.9 4.0 %collective-permute-start.5 = (s32[128]{0:T(128)S(1)}, s32[128]{0:T(128)S(1)}, u32[]{:S(2)}, u32[]{:S(2)}) collective-permute-start(s32[128]{0:T(128)S(1)} %broadcast_add_fusion.3), channel_id=1, source_target_pairs={{0,4},{4,8},{8,12},{12,16},{16,20},{20,24},{24,28},{1,5},{5,9},{9,... | collective-permute-start | bytes 1544 | tf_op jit(solution)/shard_map/ppermute | solution.py:15
  11.9 3.2 %collective-permute-start.4 = (s32[128]{0:T(128)S(1)}, s32[128]{0:T(128)S(1)}, u32[]{:S(2)}, u32[]{:S(2)}) collective-permute-start(s32[128]{0:T(128)S(1)} %broadcast_add_fusion.3), channel_id=1, source_target_pairs={{0,8},{4,12},{8,16},{12,20},{16,24},{20,28},{1,9},{5,13},{9,17},{1... | collective-permute-start | bytes 1544 | tf_op jit(solution)/shard_map/ppermute | solution.py:15
  15.1 4.2 %collective-permute-start.3 = (s32[128]{0:T(128)S(1)}, s32[128]{0:T(128)S(1)}, u32[]{:S(2)}, u32[]{:S(2)}) collective-permute-start(s32[128]{0:T(128)S(1)} %broadcast_add_fusion.3), channel_id=1, source_target_pairs={{0,12},{4,16},{8,20},{12,24},{16,28},{1,13},{5,17},{9,21},{13,25},... | collective-permute-start | bytes 1544 | tf_op jit(solution)/shard_map/ppermute | solution.py:15
  19.2 7.3 %all_gather.6 = bf16[128,1024]{1,0:T(8,128)(2,1)S(1)} all-gather(bf16[128,256]{1,0:T(8,128)(2,1)} %param.7), channel_id=1, replica_groups=mesh['seq'=8,'head'=4] {'head'}, dimensions={1}, use_global_device_ids=true | all-gather | bytes 327680 | tf_op jit(solution)/shard_map/all_gather | solution.py:55
  26.6 3.1 %collective-permute-start.2 = (bf16[128,1024]{1,0:T(8,128)(2,1)S(1)}, bf16[128,1024]{1,0:T(8,128)(2,1)S(1)}, u32[]{:S(2)}, u32[]{:S(2)}) collective-permute-start(bf16[128,1024]{1,0:T(8,128)(2,1)S(1)} %all_gather.6), channel_id=1, source_target_pairs={{0,4},{4,8},{8,12},{12,16},{16,20},{20,24},{24,28},{1,5},{5,9},{9,... | collective-permute-start | bytes 786440 | tf_op jit(solution)/shard_map/ppermute | solution.py:15
  32.0 6.1 %all_gather.7 = bf16[128,1024]{0,1:T(8,128)(2,1)S(1)} all-gather(bf16[128,256]{0,1:T(8,128)(2,1)S(1)} %copy.23), channel_id=1, replica_groups=mesh['seq'=8,'head'=4] {'head'}, dimensions={1}, use_global_device_ids=true | all-gather | bytes 327680 | tf_op jit(solution)/shard_map/all_gather | solution.py:54
  42.0 2.3 %collective-permute-start = (bf16[128,1024]{1,0:T(8,128)(2,1)S(1)}, bf16[128,1024]{1,0:T(8,128)(2,1)S(1)}, u32[]{:S(2)}, u32[]{:S(2)}) collective-permute-start(bf16[128,1024]{1,0:T(8,128)(2,1)S(1)} %all_gather.6), channel_id=1, source_target_pairs={{0,12},{4,16},{8,20},{12,24},{16,28},{1,13},{5,17},{9,21},{13,25},... | collective-permute-start | bytes 786440 | tf_op jit(solution)/shard_map/ppermute | solution.py:15
  44.3 2.6 %collective-permute-start.8 = (bf16[128,1024]{0,1:T(8,128)(2,1)S(1)}, bf16[128,1024]{0,1:T(8,128)(2,1)}, u32[]{:S(2)}, u32[]{:S(2)}) collective-permute-start(bf16[128,1024]{0,1:T(8,128)(2,1)S(1)} %all_gather.7), channel_id=1, source_target_pairs={{0,4},{4,8},{8,12},{12,16},{16,20},{20,24},{24,28},{1,5},{5,9},{9,... | collective-permute-start | bytes 786440 | tf_op jit(solution)/shard_map/ppermute | solution.py:15
  46.9 2.3 %collective-permute-start.7 = (bf16[128,1024]{0,1:T(8,128)(2,1)S(1)}, bf16[128,1024]{0,1:T(8,128)(2,1)}, u32[]{:S(2)}, u32[]{:S(2)}) collective-permute-start(bf16[128,1024]{0,1:T(8,128)(2,1)S(1)} %all_gather.7), channel_id=1, source_target_pairs={{0,8},{4,12},{8,16},{12,20},{16,24},{20,28},{1,9},{5,13},{9,17},{1... | collective-permute-start | bytes 786440 | tf_op jit(solution)/shard_map/ppermute | solution.py:15
  55.5 5.6 %collective-permute-done.6 = bf16[128,1024]{0,1:T(8,128)(2,1)} collective-permute-done((bf16[128,1024]{0,1:T(8,128)(2,1)S(1)}, bf16[128,1024]{0,1:T(8,128)(2,1)}, u32[]{:S(2)}, u32[]{:S(2)}) %collective-permute-start.6) | collective-permute-done | bytes 262176 | tf_op jit(solution)/shard_map/ppermute | solution.py:15
  62.3 3.7 %fusion.33 = (f32[8,2,128]{2,1,0:T(2,128)S(1)}, f32[8,2,128,512]{2,3,1,0:T(8,128)}) fusion(pred[128,512]{0,1:T(8,128)(4,1)S(1)} %fusion.24, bf16[512,8,128,1]{0,2,3,1:T(8,128)(2,1)S(1)} %bitcast.93, bf16[128,2,8,128]{0,3,1,2:T(8,128)(2,1)S(1)} %copy.33), kind=kOutput, calls=%fused_computation.50 | convolution fusion | flops 273678848 | bytes 5840896 | tf_op jit(solution)/shard_map/sub | solution.py:30
  66.0 3.0 %convolution_bitcast_fusion = f32[512,8,128]{0,2,1:T(8,128)S(1)} fusion(bf16[128,2,8,128]{0,3,1,2:T(8,128)(2,1)S(1)} %copy.36, f32[8,2,128,512]{2,3,1,0:T(8,128)} %get-tuple-element.15, f32[8,2,128]{2,1,0:T(2,128)S(1)} %get-tuple-element.14), kind=kOutput, calls=%fused_computation.18 | convolution fusion | flops 270532608 | bytes 6823936 | tf_op jit(solution)/shard_map/grtu,trgd->ugd/dot_general | solution.py:43
  74.3 2.7 %fusion.34 = f32[8,512,128,2]{2,1,3,0:T(8,128)} fusion(bf16[512,8,128,1]{0,2,3,1:T(8,128)(2,1)S(1)} %bitcast.87, bf16[128,2,8,128]{0,3,1,2:T(8,128)(2,1)S(1)} %copy.36), kind=kOutput, calls=%fused_computation.51 | convolution fusion | flops 268435456 | bytes 5767168 | tf_op jit(solution)/shard_map/trgd,ugd->grtu/dot_general | solution.py:36
  77.0 7.3 %fusion.12 = f32[512,8,128]{0,2,1:T(8,128)S(1)} fusion(bf16[128,2,8,128]{0,3,1,2:T(8,128)(2,1)} %copy-done.3, f32[8,512,128,2]{2,1,3,0:T(8,128)} %fusion.34, f32[8,2,128,512]{2,3,1,0:T(8,128)} %get-tuple-element.15, f32[8,2,128]{2,1,0:T(2,128)S(1)} %get-tuple-element.14), kind=kOutput, calls=%fused_computation.17 | convolution fusion | flops 275778048 | bytes 11018240 | tf_op jit(solution)/shard_map/grtu,trgd->ugd/dot_general | solution.py:42
  84.3 5.6 %collective-permute-done.12 = f32[128,8,128]{0,2,1:T(8,128)} collective-permute-done((f32[128,8,128]{0,2,1:T(8,128)}, f32[128,8,128]{0,2,1:T(8,128)}, u32[]{:S(2)}, u32[]{:S(2)}) %collective-permute-start.12) | collective-permute-done | bytes 524320 | tf_op jit(solution)/shard_map/ppermute | solution.py:15
  89.8 13.3 %collective-permute-done.14 = f32[128,8,128]{0,2,1:T(8,128)} collective-permute-done((f32[128,8,128]{0,2,1:T(8,128)}, f32[128,8,128]{0,2,1:T(8,128)}, u32[]{:S(2)}, u32[]{:S(2)}) %collective-permute-start.14) | collective-permute-done | bytes 524320 | tf_op jit(solution)/shard_map/ppermute | solution.py:15
  103.2 2.4 %fusion.19 = f32[128,8,128]{0,2,1:T(8,128)} fusion(f32[128,8,128]{0,2,1:T(8,128)} %collective-permute-done.14, f32[128,8,128]{0,2,1:T(8,128)} %collective-permute-done.13, f32[128,8,128]{0,2,1:T(8,128)} %collective-permute-done.12, f32[512,8,128]{0,2,1:T(8,128)} %copy-done), kind=kLoop, calls=%fused_computation.29 | loop fusion | flops 393216 | bytes 2621440 | tf_op jit(solution)/shard_map/add | solution.py:86
  105.6 2.1 copy.37
  111.8 30.0 %collective-permute-done.9 = f32[128,8,128]{0,2,1:T(8,128)S(1)} collective-permute-done((f32[128,8,128]{0,2,1:T(8,128)S(1)}, f32[128,8,128]{0,2,1:T(8,128)S(1)}, u32[]{:S(2)}, u32[]{:S(2)}) %collective-permute-start.9) | collective-permute-done | bytes 524320 | tf_op jit(solution)/shard_map/ppermute | solution.py:15
  141.8 14.4 %collective-permute-done.11 = f32[128,8,128]{0,2,1:T(8,128)S(1)} collective-permute-done((f32[128,8,128]{0,2,1:T(8,128)S(1)}, f32[128,8,128]{0,2,1:T(8,128)S(1)}, u32[]{:S(2)}, u32[]{:S(2)}) %collective-permute-start.11) | collective-permute-done | bytes 524320 | tf_op jit(solution)/shard_map/ppermute | solution.py:15
  156.2 9.4 %collective-permute-done.10 = f32[128,8,128]{0,2,1:T(8,128)S(1)} collective-permute-done((f32[128,8,128]{0,2,1:T(8,128)S(1)}, f32[128,8,128]{0,2,1:T(8,128)S(1)}, u32[]{:S(2)}, u32[]{:S(2)}) %collective-permute-start.10) | collective-permute-done | bytes 524320 | tf_op jit(solution)/shard_map/ppermute | solution.py:15
  168.6 2.7 %fusion.15 = bf16[128,2,8,128]{0,3,1,2:T(8,128)(2,1)S(1)} fusion(bf16[512,8,128,1]{0,2,3,1:T(8,128)(2,1)S(1)} %bitcast.88, f32[8,2,128,512]{2,3,1,0:T(8,128)} %get-tuple-element.15, f32[8,2,128]{2,1,0:T(2,128)S(1)} %get-tuple-element.14), kind=kOutput, calls=%fused_computation.22 | convolution fusion | flops 270794752 | bytes 5775360 | tf_op jit(solution)/shard_map/grtu,ugd->trgd/dot_general | solution.py:33
  172.5 7.2 %fusion.14 = bf16[128,2,8,128]{0,3,1,2:T(8,128)(2,1)S(1)} fusion(bf16[512,8,128,1]{0,2,3,1:T(8,128)(2,1)S(1)} %bitcast.94, f32[8,512,128,2]{2,1,3,0:T(8,128)} %fusion.34, f32[8,2,128,512]{2,3,1,0:T(8,128)} %get-tuple-element.15, f32[8,2,128]{2,1,0:T(2,128)S(1)} %get-tuple-element.14), kind=kOutput, calls=%fused_computation.21 | convolution fusion | flops 276040192 | bytes 9969664 | tf_op jit(solution)/shard_map/grtu,ugd->trgd/dot_general | solution.py:39
  182.5 27.3 %reduce-scatter.3.cloned.1.call-done = f32[128,256]{1,0:T(8,128)} async-done(((f32[128,1024]{1,0:T(8,128)}), f32[128,256]{1,0:T(8,128)}) %reduce-scatter.3.cloned.1.call-update) | async-done | bytes 131088 | tf_op jit(solution)/shard_map/reduce_scatter | solution.py:88
  (59 shorter events, 32.1 us)
Async XLA Ops:
  7.2 42.0 %copy-start.5 = (s32[128]{0:T(128)S(1)}, s32[128]{0:T(128)}, u32[]{:S(2)}) copy-start(s32[128]{0:T(128)} %param.9) | copy-start | bytes 1540
  7.2 173.8 %reduce-scatter.5.cloned.1.call-start = ((), (), s32[]{:S(2)}) async-start(), calls=%async_computation.3 | async-start | bytes 655360 | tf_op jit(solution)/shard_map/reduce_scatter | solution.py:91
  7.9 34.1 %collective-permute-start.5 = (s32[128]{0:T(128)S(1)}, s32[128]{0:T(128)S(1)}, u32[]{:S(2)}, u32[]{:S(2)}) collective-permute-start(s32[128]{0:T(128)S(1)} %broadcast_add_fusion.3), channel_id=1, source_target_pairs={{0,4},{4,8},{8,12},{12,16},{16,20},{20,24},{24,28},{1,5},{5,9},{9,... | collective-permute-start | bytes 1544 | tf_op jit(solution)/shard_map/ppermute | solution.py:15
  11.9 32.4 %collective-permute-start.4 = (s32[128]{0:T(128)S(1)}, s32[128]{0:T(128)S(1)}, u32[]{:S(2)}, u32[]{:S(2)}) collective-permute-start(s32[128]{0:T(128)S(1)} %broadcast_add_fusion.3), channel_id=1, source_target_pairs={{0,8},{4,12},{8,16},{12,20},{16,24},{20,28},{1,9},{5,13},{9,17},{1... | collective-permute-start | bytes 1544 | tf_op jit(solution)/shard_map/ppermute | solution.py:15
  15.1 31.8 %collective-permute-start.3 = (s32[128]{0:T(128)S(1)}, s32[128]{0:T(128)S(1)}, u32[]{:S(2)}, u32[]{:S(2)}) collective-permute-start(s32[128]{0:T(128)S(1)} %broadcast_add_fusion.3), channel_id=1, source_target_pairs={{0,12},{4,16},{8,20},{12,24},{16,28},{1,13},{5,17},{9,21},{13,25},... | collective-permute-start | bytes 1544 | tf_op jit(solution)/shard_map/ppermute | solution.py:15
  26.6 22.6 %collective-permute-start.2 = (bf16[128,1024]{1,0:T(8,128)(2,1)S(1)}, bf16[128,1024]{1,0:T(8,128)(2,1)S(1)}, u32[]{:S(2)}, u32[]{:S(2)}) collective-permute-start(bf16[128,1024]{1,0:T(8,128)(2,1)S(1)} %all_gather.6), channel_id=1, source_target_pairs={{0,4},{4,8},{8,12},{12,16},{16,20},{20,24},{24,28},{1,5},{5,9},{9,... | collective-permute-start | bytes 786440 | tf_op jit(solution)/shard_map/ppermute | solution.py:15
  29.8 21.5 %collective-permute-start.1 = (bf16[128,1024]{1,0:T(8,128)(2,1)S(1)}, bf16[128,1024]{1,0:T(8,128)(2,1)S(1)}, u32[]{:S(2)}, u32[]{:S(2)}) collective-permute-start(bf16[128,1024]{1,0:T(8,128)(2,1)S(1)} %all_gather.6), channel_id=1, source_target_pairs={{0,8},{4,12},{8,16},{12,20},{16,24},{20,28},{1,9},{5,13},{9,17},{1... | collective-permute-start | bytes 786440 | tf_op jit(solution)/shard_map/ppermute | solution.py:15
  39.9 22.4 %copy-start.3 = (bf16[128,2,8,128]{0,3,1,2:T(8,128)(2,1)}, bf16[128,2,8,128]{0,3,1,2:T(8,128)(2,1)S(1)}, u32[]{:S(2)}) copy-start(bf16[128,2,8,128]{0,3,1,2:T(8,128)(2,1)S(1)} %copy.33) | copy-start | bytes 1572868
  42.0 10.0 %collective-permute-start = (bf16[128,1024]{1,0:T(8,128)(2,1)S(1)}, bf16[128,1024]{1,0:T(8,128)(2,1)S(1)}, u32[]{:S(2)}, u32[]{:S(2)}) collective-permute-start(bf16[128,1024]{1,0:T(8,128)(2,1)S(1)} %all_gather.6), channel_id=1, source_target_pairs={{0,12},{4,16},{8,20},{12,24},{16,28},{1,13},{5,17},{9,21},{13,25},... | collective-permute-start | bytes 786440 | tf_op jit(solution)/shard_map/ppermute | solution.py:15
  44.3 9.3 %collective-permute-start.8 = (bf16[128,1024]{0,1:T(8,128)(2,1)S(1)}, bf16[128,1024]{0,1:T(8,128)(2,1)}, u32[]{:S(2)}, u32[]{:S(2)}) collective-permute-start(bf16[128,1024]{0,1:T(8,128)(2,1)S(1)} %all_gather.7), channel_id=1, source_target_pairs={{0,4},{4,8},{8,12},{12,16},{16,20},{20,24},{24,28},{1,5},{5,9},{9,... | collective-permute-start | bytes 786440 | tf_op jit(solution)/shard_map/ppermute | solution.py:15
  46.9 8.6 %collective-permute-start.7 = (bf16[128,1024]{0,1:T(8,128)(2,1)S(1)}, bf16[128,1024]{0,1:T(8,128)(2,1)}, u32[]{:S(2)}, u32[]{:S(2)}) collective-permute-start(bf16[128,1024]{0,1:T(8,128)(2,1)S(1)} %all_gather.7), channel_id=1, source_target_pairs={{0,8},{4,12},{8,16},{12,20},{16,24},{20,28},{1,9},{5,13},{9,17},{1... | collective-permute-start | bytes 786440 | tf_op jit(solution)/shard_map/ppermute | solution.py:15
  49.2 11.9 %collective-permute-start.6 = (bf16[128,1024]{0,1:T(8,128)(2,1)S(1)}, bf16[128,1024]{0,1:T(8,128)(2,1)}, u32[]{:S(2)}, u32[]{:S(2)}) collective-permute-start(bf16[128,1024]{0,1:T(8,128)(2,1)S(1)} %all_gather.7), channel_id=1, source_target_pairs={{0,12},{4,16},{8,20},{12,24},{16,28},{1,13},{5,17},{9,21},{13,25},... | collective-permute-start | bytes 786440 | tf_op jit(solution)/shard_map/ppermute | solution.py:15
  51.3 0.7 copy-start.4
  62.3 3.7 %copy-start.1 = (bf16[512,1024]{0,1:T(8,128)(2,1)}, bf16[512,1024]{0,1:T(8,128)(2,1)S(1)}, u32[]{:S(2)}) copy-start(bf16[512,1024]{0,1:T(8,128)(2,1)S(1)} %pad_maximum_fusion.1) | copy-start | bytes 3145732
  69.0 5.2 %copy-start = (f32[512,8,128]{0,2,1:T(8,128)}, f32[512,8,128]{0,2,1:T(8,128)S(1)}, u32[]{:S(2)}) copy-start(f32[512,8,128]{0,2,1:T(8,128)S(1)} %convolution_bitcast_fusion) | copy-start | bytes 6291460
  70.4 19.5 %collective-permute-start.12 = (f32[128,8,128]{0,2,1:T(8,128)}, f32[128,8,128]{0,2,1:T(8,128)}, u32[]{:S(2)}, u32[]{:S(2)}) collective-permute-start(f32[128,8,128]{0,2,1:T(8,128)} %get-tuple-element.8), channel_id=1, source_target_pairs={{4,0},{8,4},{12,8},{16,12},{20,16},{24,20},{28,24},{5,1},{9,5},{13... | collective-permute-start | bytes 1572872 | tf_op jit(solution)/shard_map/ppermute | solution.py:15
  71.7 31.5 %collective-permute-start.14 = (f32[128,8,128]{0,2,1:T(8,128)}, f32[128,8,128]{0,2,1:T(8,128)}, u32[]{:S(2)}, u32[]{:S(2)}) collective-permute-start(f32[128,8,128]{0,2,1:T(8,128)} %get-tuple-element.9), channel_id=1, source_target_pairs={{12,0},{16,4},{20,8},{24,12},{28,16},{13,1},{17,5},{21,9},{25,13},... | collective-permute-start | bytes 1572872 | tf_op jit(solution)/shard_map/ppermute | solution.py:15
  73.0 30.2 %collective-permute-start.13 = (f32[128,8,128]{0,2,1:T(8,128)}, f32[128,8,128]{0,2,1:T(8,128)}, u32[]{:S(2)}, u32[]{:S(2)}) collective-permute-start(f32[128,8,128]{0,2,1:T(8,128)} %get-tuple-element.10), channel_id=1, source_target_pairs={{8,0},{12,4},{16,8},{20,12},{24,16},{28,20},{9,1},{13,5},{17,9},{2... | collective-permute-start | bytes 1572872 | tf_op jit(solution)/shard_map/ppermute | solution.py:15
  107.7 102.1 %reduce-scatter.3.cloned.1.call-start = ((), (), s32[]{:S(2)}) async-start(), calls=%async_computation.2 | async-start | bytes 655360 | tf_op jit(solution)/shard_map/reduce_scatter | solution.py:88
  107.9 33.9 %collective-permute-start.9 = (f32[128,8,128]{0,2,1:T(8,128)S(1)}, f32[128,8,128]{0,2,1:T(8,128)S(1)}, u32[]{:S(2)}, u32[]{:S(2)}) collective-permute-start(f32[128,8,128]{0,2,1:T(8,128)S(1)} %get-tuple-element.11), channel_id=1, source_target_pairs={{4,0},{8,4},{12,8},{16,12},{20,16},{24,20},{28,24},{5,1},{9,5},{13... | collective-permute-start | bytes 1572872 | tf_op jit(solution)/shard_map/ppermute | solution.py:15
  109.2 46.9 %collective-permute-start.11 = (f32[128,8,128]{0,2,1:T(8,128)S(1)}, f32[128,8,128]{0,2,1:T(8,128)S(1)}, u32[]{:S(2)}, u32[]{:S(2)}) collective-permute-start(f32[128,8,128]{0,2,1:T(8,128)S(1)} %get-tuple-element.12), channel_id=1, source_target_pairs={{12,0},{16,4},{20,8},{24,12},{28,16},{13,1},{17,5},{21,9},{25,13},... | collective-permute-start | bytes 1572872 | tf_op jit(solution)/shard_map/ppermute | solution.py:15
  110.5 55.1 %collective-permute-start.10 = (f32[128,8,128]{0,2,1:T(8,128)S(1)}, f32[128,8,128]{0,2,1:T(8,128)S(1)}, u32[]{:S(2)}, u32[]{:S(2)}) collective-permute-start(f32[128,8,128]{0,2,1:T(8,128)S(1)} %get-tuple-element.13), channel_id=1, source_target_pairs={{8,0},{12,4},{16,8},{20,12},{24,16},{28,20},{9,1},{13,5},{17,9},{2... | collective-permute-start | bytes 1572872 | tf_op jit(solution)/shard_map/ppermute | solution.py:15
  168.6 3.9 %copy-start.2 = (bf16[512,1024]{0,1:T(8,128)(2,1)S(1)}, bf16[512,1024]{0,1:T(8,128)(2,1)}, u32[]{:S(2)}) copy-start(bf16[512,1024]{0,1:T(8,128)(2,1)} %copy-done.1) | copy-start | bytes 3145732
Sparse Core Ops, SparseCore 0:
  107.8 52.4 reduce-scatter.4
  168.7 40.9 reduce-scatter.2
where the time goes:
time: 220 us; the launch traced here: 218 us
  waiting for transfers between devices  107 us (49%)
  starting transfers between devices  32.7 us (15%)
  matrix products  26.7 us (12%)
  between operations  14.4 us (7%)
  local copies, waits for them, and re-layouts  14 us (6%)
  blocking collectives  13.4 us (6%)
  other arithmetic  9.49 us (4%)
    ppermute x15, waiting for transfers between devices, passed_along(): lax.ppermute(value, axis, [(source, source + steps) for source in range(l...  80.2 us
    ppermute x15, starting transfers between devices, passed_along(): lax.ppermute(value, axis, [(source, source + steps) for source in range(l...  32.6 us
    reduce_scatter x1, waiting for transfers between devices, on_device(): lax.psum_scatter(total_keys.reshape(rows_n, groups_total * HD), 'head', s...  27.3 us
    all_gather x1, blocking collectives, on_device(): lax.all_gather(values, 'head', axis=1, tiled=True)  7.35 us
    dot_general x1, matrix products, attend(): jnp.einsum('grtu,trgd->ugd', dscore, query_blk, preferred_element_type=jn...  7.27 us
    dot_general x1, matrix products, attend(): jnp.einsum('grtu,ugd->trgd', dscore, key_win, preferred_element_type=jnp....  7.24 us
    all_gather x1, blocking collectives, on_device(): lax.all_gather(keys, 'head', axis=1, tiled=True)  6.07 us
  transfers between devices with their start and end apart: 17, of which 8 were waited for; matrix products, arithmetic and copies ran while one was open for 15% of the time, Pallas kernels for 0%

commit v1 on v0

v1 whole, which is shorter than its diff:
```python
import functools
import math

import jax
import jax.numpy as jnp
from jax import lax
from jax.experimental import pallas as pl
from jax.experimental.pallas import tpu as pltpu
from jax.sharding import PartitionSpec as P

HD = 128
REACH = 3
MESH = pl.DeviceIdType.MESH


def partner(index, bits):
    out = index
    place = 1
    while place <= bits:
        if bits & place:
            out = out + place * (1 - 2 * ((index // place) % 2))
        place *= 2
    return out


def kernel(
    n_seq, n_head, reps,
    q_ref, k_ref, v_ref, g_ref, doc_ref,
    att_ref, qg_ref, kg_ref, vg_ref,
    qbuf, gbuf, kwin, vwin, kt, vt, docwin, bias, attbuf, qgbuf, kacc, vacc,
    kg_out, vg_out, kg_in, vg_in,
    halo_send, halo_recv, in_send, in_recv, ret_send, ret_recv, grad_send, grad_recv, local_sem,
):
    seq, head = lax.axis_index("seq"), lax.axis_index("head")
    tok, cols = k_ref.shape
    rows = q_ref.shape[0]
    groups = cols // HD
    steps = range(1, REACH + 1)
    peers = range(1, n_head)

    def block(b):
        return pl.ds(b * tok, tok)

    def lanes(g):
        return pl.ds(g * HD, HD)

    def columns(owner, g):
        return pl.ds(pl.multiple_of(owner * cols + g * HD, HD), HD)

    halo = {}
    for b in steps:
        for i, (src, dst) in enumerate(
            ((k_ref, kwin.at[block(b)]), (v_ref, vwin.at[block(b)]), (doc_ref, docwin.at[b]))
        ):
            halo[b, i] = pltpu.make_async_remote_copy(
                src_ref=src, dst_ref=dst, send_sem=halo_send.at[b - 1, i],
                recv_sem=halo_recv.at[b - 1, i], device_id=(seq + b, head), device_id_type=MESH)
    inward = {}
    outward = {}
    for d in peers:
        other = partner(head, d)
        for g in range(groups):
            for i, (src, dst) in enumerate(((q_ref, qbuf), (g_ref, gbuf))):
                inward[d, g, i] = pltpu.make_async_remote_copy(
                    src_ref=src.at[:, columns(other, g)], dst_ref=dst.at[d, :, lanes(g)],
                    send_sem=in_send.at[d - 1, g, i], recv_sem=in_recv.at[d - 1, g, i],
                    device_id=(seq, other), device_id_type=MESH)
            for i, (src, dst) in enumerate(((attbuf, att_ref), (qgbuf, qg_ref))):
                outward[d, g, i] = pltpu.make_async_remote_copy(
                    src_ref=src.at[d, :, lanes(g)], dst_ref=dst.at[:, columns(head, g)],
                    send_sem=ret_send.at[d - 1, g, i], recv_sem=ret_recv.at[d - 1, g, i],
                    device_id=(seq, other), device_id_type=MESH)
    back = {}
    for b in steps:
        for g in range(groups):
            for i, (src, dst) in enumerate(((vg_out, vg_in), (kg_out, kg_in))):
                back[b, g, i] = pltpu.make_async_remote_copy(
                    src_ref=src.at[b - 1, :, lanes(g)], dst_ref=dst.at[b - 1, :, lanes(g)],
                    send_sem=grad_send.at[b - 1, g, i], recv_sem=grad_recv.at[b - 1, g, i],
                    device_id=(seq - b, head), device_id_type=MESH)

    barrier = pltpu.get_barrier_semaphore()
    for d in peers:
        pl.semaphore_signal(barrier, 1, device_id=(seq, partner(head, d)), device_id_type=MESH)
    count = n_head - 1
    for b in steps:
        @pl.when(seq + b < n_seq)
        def _():
            pl.semaphore_signal(barrier, 1, device_id=(seq + b, head), device_id_type=MESH)

        @pl.when(seq >= b)
        def _():
            pl.semaphore_signal(barrier, 1, device_id=(seq - b, head), device_id_type=MESH)
        count = count + jnp.where(seq + b < n_seq, 1, 0) + jnp.where(seq >= b, 1, 0)

    own = [
        pltpu.make_async_copy(src, dst, local_sem.at[i])
        for i, (src, dst) in enumerate((
            (k_ref, kwin.at[block(0)]), (v_ref, vwin.at[block(0)]), (doc_ref, docwin.at[0]),
            (q_ref.at[:, pl.ds(pl.multiple_of(head * cols, HD), cols)], qbuf.at[0]),
            (g_ref.at[:, pl.ds(pl.multiple_of(head * cols, HD), cols)], gbuf.at[0])))
    ]
    for copy in own:
        copy.start()
    pl.semaphore_wait(barrier, count)

    for b in steps:
        @pl.when(seq + b < n_seq)
        def _():
            for i in (2, 0, 1):
                halo[b, i].start()
    for d in peers:
        for g in range(groups):
            for i in range(2):
                inward[d, g, i].start()

    for b in steps:
        @pl.when(seq < b)
        def _():
            kwin[block(b), :] = jnp.zeros((tok, cols), kwin.dtype)
            vwin[block(b), :] = jnp.zeros((tok, cols), vwin.dtype)
            docwin[b] = jnp.full((1, tok), -1, jnp.int32)

    key_of = lax.broadcasted_iota(jnp.int32, (tok, rows), 0)
    token_of = lax.broadcasted_iota(jnp.int32, (tok, rows), 1) // reps
    near = key_of <= token_of
    for copy in own:
        copy.wait()
    for b in steps:
        @pl.when(seq >= b)
        def _():
            for i in range(3):
                halo[b, i].wait_recv()

    doc_own = docwin[0].astype(jnp.float32)
    if reps == 1:
        doc_q = doc_own
    else:
        spread = (key_of == token_of).astype(jnp.bfloat16)
        doc_q = jnp.dot(jnp.broadcast_to(doc_own, (16, tok)).astype(jnp.bfloat16), spread,
                        preferred_element_type=jnp.float32)[0:1]

    def same(b):
        doc = jnp.transpose(jnp.broadcast_to(docwin[b].astype(jnp.float32), (tok, tok)))
        return jnp.where(doc[:, 0:1] == doc_q, 0.0, -1e30)

    bias[block(0), :] = jnp.where(near, same(0), same(REACH))
    for b in range(1, REACH):
        bias[block(b), :] = same(b)
    for g in range(groups):
        kt[g] = jnp.transpose(kwin[:, lanes(g)])
        vt[g] = jnp.transpose(vwin[:, lanes(g)])

    scale = 1.0 / math.sqrt(HD)
    last = REACH * tok

    def folded(x):
        return jnp.concatenate([jnp.where(near, x[:tok], x[last:]), x[tok:last]], axis=0)

    def unfolded(x):
        zero = jnp.zeros((tok, rows), x.dtype)
        return jnp.concatenate(
            [jnp.where(near, x[:tok], zero), x[tok:], jnp.where(near, zero, x[:tok])], axis=0)

    def tile(d, g):
        q = qbuf[d, :, lanes(g)]
        grad = gbuf[d, :, lanes(g)]
        by_last = (((1,), (1,)), ((), ()))
        s = folded(lax.dot_general(kwin[:, lanes(g)], q, by_last, preferred_element_type=jnp.float32))
        s = s + bias[...]
        top = jnp.max(s, axis=0, keepdims=True)
        e = jnp.exp2((s - top) * (scale * math.log2(math.e)))
        p = e * (1.0 / jnp.sum(e, axis=0, keepdims=True))
        dp = folded(lax.dot_general(vwin[:, lanes(g)], grad, by_last, preferred_element_type=jnp.float32))
        delta = jnp.sum(p * dp, axis=0, keepdims=True)
        ds = unfolded(p * (dp - delta) * scale).astype(jnp.bfloat16)
        pb = unfolded(p).astype(jnp.bfloat16)
        att = jnp.dot(vt[g], pb, preferred_element_type=jnp.float32)
        attbuf[d, :, lanes(g)] = jnp.transpose(att).astype(jnp.bfloat16)
        qg = jnp.dot(kt[g], ds, preferred_element_type=jnp.float32)
        qgbuf[d, :, lanes(g)] = jnp.transpose(qg).astype(jnp.bfloat16)
        dv = jnp.dot(pb, grad, preferred_element_type=jnp.float32)
        dk = jnp.dot(ds, q, preferred_element_type=jnp.float32)
        if d == 0:
            vacc[:, lanes(g)] = dv
            kacc[:, lanes(g)] = dk
        else:
            vacc[:, lanes(g)] += dv
            kacc[:, lanes(g)] += dk

    for d in range(n_head):
        for g in range(groups):
            if d:
                inward[d, g, 0].wait_recv()
                inward[d, g, 1].wait_recv()
            tile(d, g)
            if d:
                outward[d, g, 0].start()
                outward[d, g, 1].start()
            if d == n_head - 1:
                for b in steps:
                    vg_out[b - 1, :, lanes(g)] = vacc[block(b), lanes(g)].astype(jnp.bfloat16)
                    kg_out[b - 1, :, lanes(g)] = kacc[block(b), lanes(g)].astype(jnp.bfloat16)

                    @pl.when(seq >= b)
                    def _():
                        back[b, g, 0].start()
                        back[b, g, 1].start()
        if d == 0:
            mine = pl.ds(pl.multiple_of(head * cols, HD), cols)
            done = [pltpu.make_async_copy(attbuf.at[0], att_ref.at[:, mine], local_sem.at[0]),
                    pltpu.make_async_copy(qgbuf.at[0], qg_ref.at[:, mine], local_sem.at[1])]
            for copy in done:
                copy.start()

    for b in steps:
        @pl.when(seq + b < n_seq)
        def _():
            for g in range(groups):
                for i in range(2):
                    back[b, g, i].wait_recv()
            vacc[block(0), :] += vg_in[b - 1].astype(jnp.float32)
            kacc[block(0), :] += kg_in[b - 1].astype(jnp.float32)
    vg_ref[...] = vacc[block(0), :].astype(vg_ref.dtype)
    kg_ref[...] = kacc[block(0), :].astype(kg_ref.dtype)

    for copy in done:
        copy.wait()
    for b in steps:
        @pl.when(seq + b < n_seq)
        def _():
            for i in range(3):
                halo[b, i].wait_send()

        @pl.when(seq >= b)
        def _():
            for g in range(groups):
                for i in range(2):
                    back[b, g, i].wait_send()
    for d in peers:
        for g in range(groups):
            for i in range(2):
                inward[d, g, i].wait_send()
                outward[d, g, i].wait_send()
                outward[d, g, i].wait_recv()


def on_device(n_seq, n_head, queries, keys, values, out_grad, doc_ids):
    tok, reps, width = queries.shape
    cols = keys.shape[1]
    groups = cols // HD
    rows = tok * reps
    span = (REACH + 1) * tok
    bf16, f32 = jnp.bfloat16, jnp.float32
    dma = pltpu.SemaphoreType.DMA
    anywhere = pl.BlockSpec(memory_space=pl.ANY)
    vmem = pl.BlockSpec(memory_space=pltpu.VMEM)
    flat = jax.ShapeDtypeStruct((rows, width), bf16)
    narrow = jax.ShapeDtypeStruct((tok, cols), bf16)
    att, qg, kg, vg = pl.pallas_call(
        functools.partial(kernel, n_seq, n_head, reps),
        out_shape=(flat, flat, narrow, narrow),
        in_specs=[anywhere] * 5,
        out_specs=(anywhere, anywhere, vmem, vmem),
        scratch_shapes=[
            pltpu.VMEM((n_head, rows, cols), bf16),
            pltpu.VMEM((n_head, rows, cols), bf16),
            pltpu.VMEM((span, cols), bf16),
            pltpu.VMEM((span, cols), bf16),
            pltpu.VMEM((groups, HD, span), bf16),
            pltpu.VMEM((groups, HD, span), bf16),
            pltpu.VMEM((REACH + 1, 1, tok), jnp.int32),
            pltpu.VMEM((REACH * tok, rows), f32),
            pltpu.VMEM((n_head, rows, cols), bf16),
            pltpu.VMEM((n_head, rows, cols), bf16),
            pltpu.VMEM((span, cols), f32),
            pltpu.VMEM((span, cols), f32),
            pltpu.VMEM((REACH, tok, cols), bf16),
            pltpu.VMEM((REACH, tok, cols), bf16),
            pltpu.VMEM((REACH, tok, cols), bf16),
            pltpu.VMEM((REACH, tok, cols), bf16),
            dma((REACH, 3)), dma((REACH, 3)),
            dma((n_head - 1, groups, 2)), dma((n_head - 1, groups, 2)),
            dma((n_head - 1, groups, 2)), dma((n_head - 1, groups, 2)),
            dma((REACH, groups, 2)), dma((REACH, groups, 2)),
            dma((5,)),
        ],
        compiler_params=pltpu.CompilerParams(
            collective_id=0, has_side_effects=True, vmem_limit_bytes=32 * 2**20),
        cost_estimate=pl.CostEstimate(
            flops=12 * n_head * groups * rows * span * HD,
            bytes_accessed=8 * rows * width + 8 * tok * cols,
            transcendentals=n_head * groups * rows * REACH * tok),
        name="attention_layer",
    )(queries.reshape(rows, width), keys, values, out_grad.reshape(rows, width), doc_ids.reshape(1, tok))
    return (att.reshape(tok, reps, width), qg.reshape(tok, reps, width), kg, vg)


def solution(mesh):
    wide, thin = P("seq", "head", None), P("seq", "head")
    return jax.shard_map(
        functools.partial(on_device, mesh.shape["seq"], mesh.shape["head"]),
        mesh=mesh, in_specs=(wide, thin, thin, wide, P("seq")),
        out_specs=(wide, wide, thin, thin), check_vma=False)
```

time: 220 us -> 39.2 us (0.18)
  the two profiles are of different devices: /device:TPU:1 before, /device:TPU:12 now
where the time goes in v1:
time: 39.2 us; the launch traced here: 39 us
  Pallas kernels  33 us (84%)
  local copies, waits for them, and re-layouts  5.39 us (14%)
  between operations  0.69 us (2%)
    pallas_call x1, Pallas kernels, on_device(): pl.pallas_call(functools.partial(kernel, n_seq, n_head, reps), out_shape=...  33 us
    reshape x2, local copies, waits for them, and re-layouts, on_device(): return (att.reshape(tok, reps, width), qg.reshape(tok, reps, width), kg, vg)  1.98 us
    unnamed x10, local copies, waits for them, and re-layouts  1.91 us
    reshape x1, local copies, waits for them, and re-layouts, on_device(): queries.reshape(rows, width)  1.3 us

profile of v1, /device:TPU:12, one launch (start us, length us, event | category | flops | bytes accessed | tf_op | source)
XLA Modules:
  0.0 39.0 jit_solution(16648494450971488395)
XLA Ops:
  0.6 0.0 copy-start.3
  0.6 1.3 %reshape.23.q_ref = bf16[256,1024]{1,0:T(8,128)(2,1)S(1)} reshape(bf16[128,2,1024]{2,1,0:T(2,128)(2,1)} %param.5) | data formatting | bytes 1048576 | tf_op jit(solution)/shard_map/reshape | solution.py:295
  1.9 0.0 copy-done.3
  2.0 0.0 copy-start
  2.0 0.0 copy-start.1
  2.0 0.0 copy-start.2
  2.0 0.2 reshape.24.g_ref
  2.2 0.6 %copy-done = bf16[128,256]{1,0:T(8,128)(2,1)S(1)} copy-done((bf16[128,256]{1,0:T(8,128)(2,1)S(1)}, bf16[128,256]{1,0:T(8,128)(2,1)}, u32[]{:S(2)}) %copy-start) | copy-done | bytes 65560
  2.8 0.0 copy-done.1
  2.8 0.0 copy-done.2
  2.8 33.0 %attention_layer.1 = (bf16[256,1024]{1,0:T(8,128)(2,1)S(1)}, bf16[256,1024]{1,0:T(8,128)(2,1)S(1)}, bf16[128,256]{1,0:T(8,128)(2,1)S(1)}, bf16[128,256]{1,0:T(8,128)(2,1)S(1)}) custom-call(bf16[256,1024]{1,0:T(8,128)(2,1)S(1)} %reshape.23.q_ref, bf16[128,256]{1,0:T(8,128)(2,1)S(1)} %copy-done, bf16[128,256]{1,0:T(8,128)(2,1)S(1)} %copy-done.1, ...), custom_call_target="tpu_custom_call" | custom-call | flops 1610612736 | bytes 2359296 | tf_op jit(solution)/shard_map/attention_layer/pallas_call | solution.py:260
  35.8 1.0 %reshape.26 = bf16[128,2,1024]{2,1,0:T(2,128)(2,1)} reshape(bf16[256,1024]{1,0:T(8,128)(2,1)S(1)} %get-tuple-element.8) | data formatting | bytes 1048576 | tf_op jit(solution)/shard_map/reshape | solution.py:296
  36.8 1.0 %reshape.27 = bf16[128,2,1024]{2,1,0:T(2,128)(2,1)} reshape(bf16[256,1024]{1,0:T(8,128)(2,1)S(1)} %get-tuple-element.9) | data formatting | bytes 1048576 | tf_op jit(solution)/shard_map/reshape | solution.py:296
  37.8 0.6 %copy.11 = bf16[128,256]{1,0:T(8,128)(2,1)} copy(bf16[128,256]{1,0:T(8,128)(2,1)S(1)} %get-tuple-element.18) | data formatting | bytes 131072
  38.4 0.6 %copy.12 = bf16[128,256]{1,0:T(8,128)(2,1)} copy(bf16[128,256]{1,0:T(8,128)(2,1)S(1)} %get-tuple-element.19) | data formatting | bytes 131072
Async XLA Ops:
  0.6 1.3 %copy-start.3 = (bf16[128,2,1024]{2,1,0:T(2,128)(2,1)S(1)}, bf16[128,2,1024]{2,1,0:T(2,128)(2,1)}, u32[]{:S(2)}) copy-start(bf16[128,2,1024]{2,1,0:T(2,128)(2,1)} %param.8) | copy-start | bytes 1572868
  2.0 0.8 %copy-start = (bf16[128,256]{1,0:T(8,128)(2,1)S(1)}, bf16[128,256]{1,0:T(8,128)(2,1)}, u32[]{:S(2)}) copy-start(bf16[128,256]{1,0:T(8,128)(2,1)} %k_ref.1) | copy-start | bytes 196612
  2.0 0.9 %copy-start.1 = (bf16[128,256]{1,0:T(8,128)(2,1)S(1)}, bf16[128,256]{1,0:T(8,128)(2,1)}, u32[]{:S(2)}) copy-start(bf16[128,256]{1,0:T(8,128)(2,1)} %v_ref.1) | copy-start | bytes 196612
  2.0 0.9 %copy-start.2 = (s32[128]{0:T(128)S(1)}, s32[128]{0:T(128)}, u32[]{:S(2)}) copy-start(s32[128]{0:T(128)} %param.9) | copy-start | bytes 1540

commit v2 on v1

--- a/solution.py
+++ b/solution.py
@@ -49,12 +49,15 @@
 
     halo = {}
     for b in steps:
-        for i, (src, dst) in enumerate(
-            ((k_ref, kwin.at[block(b)]), (v_ref, vwin.at[block(b)]), (doc_ref, docwin.at[b]))
-        ):
+        pairs = [(doc_ref, docwin.at[b])]
+        for g in range(groups):
+            pairs.append((k_ref.at[:, lanes(g)], kwin.at[block(b), lanes(g)]))
+            pairs.append((v_ref.at[:, lanes(g)], vwin.at[block(b), lanes(g)]))
+        for i, (src, dst) in enumerate(pairs):
             halo[b, i] = pltpu.make_async_remote_copy(
                 src_ref=src, dst_ref=dst, send_sem=halo_send.at[b - 1, i],
                 recv_sem=halo_recv.at[b - 1, i], device_id=(seq + b, head), device_id_type=MESH)
+    halos = 1 + 2 * groups
     inward = {}
     outward = {}
     for d in peers:
@@ -104,13 +107,13 @@
         copy.start()
     pl.semaphore_wait(barrier, count)
 
-    for b in steps:
-        @pl.when(seq + b < n_seq)
-        def _():
-            for i in (2, 0, 1):
-                halo[b, i].start()
-    for d in peers:
-        for g in range(groups):
+    for g in range(groups):
+        for b in reversed(steps):
+            @pl.when(seq + b < n_seq)
+            def _():
+                for i in ((0, 1, 2) if g == 0 else (1 + 2 * g, 2 + 2 * g)):
+                    halo[b, i].start()
+        for d in reversed(peers):
             for i in range(2):
                 inward[d, g, i].start()
 
@@ -129,8 +132,7 @@
     for b in steps:
         @pl.when(seq >= b)
         def _():
-            for i in range(3):
-                halo[b, i].wait_recv()
+            halo[b, 0].wait_recv()
 
     doc_own = docwin[0].astype(jnp.float32)
     if reps == 1:
@@ -147,9 +149,6 @@
     bias[block(0), :] = jnp.where(near, same(0), same(REACH))
     for b in range(1, REACH):
         bias[block(b), :] = same(b)
-    for g in range(groups):
-        kt[g] = jnp.transpose(kwin[:, lanes(g)])
-        vt[g] = jnp.transpose(vwin[:, lanes(g)])
 
     scale = 1.0 / math.sqrt(HD)
     last = REACH * tok
@@ -188,8 +187,18 @@
             vacc[:, lanes(g)] += dv
             kacc[:, lanes(g)] += dk
 
-    for d in range(n_head):
-        for g in range(groups):
+    mine = pl.ds(pl.multiple_of(head * cols, HD), cols)
+    done = [pltpu.make_async_copy(attbuf.at[0], att_ref.at[:, mine], local_sem.at[0]),
+            pltpu.make_async_copy(qgbuf.at[0], qg_ref.at[:, mine], local_sem.at[1])]
+    for g in range(groups):
+        for b in steps:
+            @pl.when(seq >= b)
+            def _():
+                halo[b, 1 + 2 * g].wait_recv()
+                halo[b, 2 + 2 * g].wait_recv()
+        kt[g] = jnp.transpose(kwin[:, lanes(g)])
+        vt[g] = jnp.transpose(vwin[:, lanes(g)])
+        for d in range(n_head):
             if d:
                 inward[d, g, 0].wait_recv()
                 inward[d, g, 1].wait_recv()
@@ -197,21 +206,17 @@
             if d:
                 outward[d, g, 0].start()
                 outward[d, g, 1].start()
-            if d == n_head - 1:
-                for b in steps:
-                    vg_out[b - 1, :, lanes(g)] = vacc[block(b), lanes(g)].astype(jnp.bfloat16)
-                    kg_out[b - 1, :, lanes(g)] = kacc[block(b), lanes(g)].astype(jnp.bfloat16)
-
-                    @pl.when(seq >= b)
-                    def _():
-                        back[b, g, 0].start()
-                        back[b, g, 1].start()
-        if d == 0:
-            mine = pl.ds(pl.multiple_of(head * cols, HD), cols)
-            done = [pltpu.make_async_copy(attbuf.at[0], att_ref.at[:, mine], local_sem.at[0]),
-                    pltpu.make_async_copy(qgbuf.at[0], qg_ref.at[:, mine], local_sem.at[1])]
-            for copy in done:
-                copy.start()
+            elif g == groups - 1:
+                for copy in done:
+                    copy.start()
+        for b in reversed(steps):
+            vg_out[b - 1, :, lanes(g)] = vacc[block(b), lanes(g)].astype(jnp.bfloat16)
+            kg_out[b - 1, :, lanes(g)] = kacc[block(b), lanes(g)].astype(jnp.bfloat16)
+
+            @pl.when(seq >= b)
+            def _():
+                back[b, g, 0].start()
+                back[b, g, 1].start()
 
     for b in steps:
         @pl.when(seq + b < n_seq)
@@ -229,7 +234,7 @@
     for b in steps:
         @pl.when(seq + b < n_seq)
         def _():
-            for i in range(3):
+            for i in range(halos):
                 halo[b, i].wait_send()
 
         @pl.when(seq >= b)
@@ -279,7 +284,7 @@
             pltpu.VMEM((REACH, tok, cols), bf16),
             pltpu.VMEM((REACH, tok, cols), bf16),
             pltpu.VMEM((REACH, tok, cols), bf16),
-            dma((REACH, 3)), dma((REACH, 3)),
+            dma((REACH, 1 + 2 * groups)), dma((REACH, 1 + 2 * groups)),
             dma((n_head - 1, groups, 2)), dma((n_head - 1, groups, 2)),
             dma((n_head - 1, groups, 2)), dma((n_head - 1, groups, 2)),
             dma((REACH, groups, 2)), dma((REACH, groups, 2)),

time: 39.2 us -> 34.9 us (0.89)
  the two profiles are of different devices: /device:TPU:12 before, /device:TPU:1 now
where the time goes in v2:
time: 34.9 us; the launch traced here: 34.8 us
  Pallas kernels  28.7 us (82%)
  local copies, waits for them, and re-layouts  5.39 us (15%)
  between operations  0.69 us (2%)
    pallas_call x1, Pallas kernels, on_device(): pl.pallas_call(functools.partial(kernel, n_seq, n_head, reps), out_shape=...  28.7 us
    reshape x2, local copies, waits for them, and re-layouts, on_device(): return (att.reshape(tok, reps, width), qg.reshape(tok, reps, width), kg, vg)  1.98 us
    unnamed x10, local copies, waits for them, and re-layouts  1.91 us
    reshape x1, local copies, waits for them, and re-layouts, on_device(): queries.reshape(rows, width)  1.3 us

profile of v2, /device:TPU:1, one launch (start us, length us, event | category | flops | bytes accessed | tf_op | source)
XLA Modules:
  0.0 34.8 jit_solution(3706842141077982324)
XLA Ops:
  0.6 0.0 copy-start.3
  0.6 1.3 %reshape.23.q_ref = bf16[256,1024]{1,0:T(8,128)(2,1)S(1)} reshape(bf16[128,2,1024]{2,1,0:T(2,128)(2,1)} %param.5) | data formatting | bytes 1048576 | tf_op jit(solution)/shard_map/reshape | solution.py:300
  1.9 0.0 copy-done.3
  2.0 0.0 copy-start
  2.0 0.0 copy-start.1
  2.0 0.0 copy-start.2
  2.0 0.2 reshape.24.g_ref
  2.2 0.6 %copy-done = bf16[128,256]{1,0:T(8,128)(2,1)S(1)} copy-done((bf16[128,256]{1,0:T(8,128)(2,1)S(1)}, bf16[128,256]{1,0:T(8,128)(2,1)}, u32[]{:S(2)}) %copy-start) | copy-done | bytes 65560
  2.8 0.0 copy-done.1
  2.8 0.0 copy-done.2
  2.8 28.7 %attention_layer.1 = (bf16[256,1024]{1,0:T(8,128)(2,1)S(1)}, bf16[256,1024]{1,0:T(8,128)(2,1)S(1)}, bf16[128,256]{1,0:T(8,128)(2,1)S(1)}, bf16[128,256]{1,0:T(8,128)(2,1)S(1)}) custom-call(bf16[256,1024]{1,0:T(8,128)(2,1)S(1)} %reshape.23.q_ref, bf16[128,256]{1,0:T(8,128)(2,1)S(1)} %copy-done, bf16[128,256]{1,0:T(8,128)(2,1)S(1)} %copy-done.1, ...), custom_call_target="tpu_custom_call" | custom-call | flops 1610612736 | bytes 2359296 | tf_op jit(solution)/shard_map/attention_layer/pallas_call | solution.py:265
  31.5 1.0 %reshape.26 = bf16[128,2,1024]{2,1,0:T(2,128)(2,1)} reshape(bf16[256,1024]{1,0:T(8,128)(2,1)S(1)} %get-tuple-element.8) | data formatting | bytes 1048576 | tf_op jit(solution)/shard_map/reshape | solution.py:301
  32.5 1.0 %reshape.27 = bf16[128,2,1024]{2,1,0:T(2,128)(2,1)} reshape(bf16[256,1024]{1,0:T(8,128)(2,1)S(1)} %get-tuple-element.9) | data formatting | bytes 1048576 | tf_op jit(solution)/shard_map/reshape | solution.py:301
  33.5 0.6 %copy.11 = bf16[128,256]{1,0:T(8,128)(2,1)} copy(bf16[128,256]{1,0:T(8,128)(2,1)S(1)} %get-tuple-element.18) | data formatting | bytes 131072
  34.1 0.6 %copy.12 = bf16[128,256]{1,0:T(8,128)(2,1)} copy(bf16[128,256]{1,0:T(8,128)(2,1)S(1)} %get-tuple-element.19) | data formatting | bytes 131072
Async XLA Ops:
  0.6 1.3 %copy-start.3 = (bf16[128,2,1024]{2,1,0:T(2,128)(2,1)S(1)}, bf16[128,2,1024]{2,1,0:T(2,128)(2,1)}, u32[]{:S(2)}) copy-start(bf16[128,2,1024]{2,1,0:T(2,128)(2,1)} %param.8) | copy-start | bytes 1572868
  2.0 0.8 %copy-start = (bf16[128,256]{1,0:T(8,128)(2,1)S(1)}, bf16[128,256]{1,0:T(8,128)(2,1)}, u32[]{:S(2)}) copy-start(bf16[128,256]{1,0:T(8,128)(2,1)} %k_ref.1) | copy-start | bytes 196612
  2.0 0.9 %copy-start.1 = (bf16[128,256]{1,0:T(8,128)(2,1)S(1)}, bf16[128,256]{1,0:T(8,128)(2,1)}, u32[]{:S(2)}) copy-start(bf16[128,256]{1,0:T(8,128)(2,1)} %v_ref.1) | copy-start | bytes 196612
  2.0 0.9 %copy-start.2 = (s32[128]{0:T(128)S(1)}, s32[128]{0:T(128)}, u32[]{:S(2)}) copy-start(s32[128]{0:T(128)} %param.9) | copy-start | bytes 1540

commit v3 on v2

--- a/solution.py
+++ b/solution.py
@@ -10,6 +10,7 @@
 
 HD = 128
 REACH = 3
+LIMIT = 60 * 2**20
 MESH = pl.DeviceIdType.MESH
 
 
@@ -33,7 +34,7 @@
 ):
     seq, head = lax.axis_index("seq"), lax.axis_index("head")
     tok, cols = k_ref.shape
-    rows = q_ref.shape[0]
+    rows = tok * reps
     groups = cols // HD
     steps = range(1, REACH + 1)
     peers = range(1, n_head)
@@ -44,8 +45,13 @@
     def lanes(g):
         return pl.ds(g * HD, HD)
 
-    def columns(owner, g):
-        return pl.ds(pl.multiple_of(owner * cols + g * HD, HD), HD)
+    def columns(ref, owner, g):
+        at = pl.ds(pl.multiple_of(owner * cols + g * HD, HD), HD)
+        return ref.at[:, at] if len(ref.shape) == 2 else ref.at[:, :, at]
+
+    def matrix(ref, d, g):
+        view = ref.at[d, g]
+        return view if len(view.shape) == 2 else view.reshape(rows, HD)
 
     halo = {}
     for b in steps:
@@ -65,12 +71,12 @@
         for g in range(groups):
             for i, (src, dst) in enumerate(((q_ref, qbuf), (g_ref, gbuf))):
                 inward[d, g, i] = pltpu.make_async_remote_copy(
-                    src_ref=src.at[:, columns(other, g)], dst_ref=dst.at[d, :, lanes(g)],
+                    src_ref=columns(src, other, g), dst_ref=dst.at[d, g],
                     send_sem=in_send.at[d - 1, g, i], recv_sem=in_recv.at[d - 1, g, i],
                     device_id=(seq, other), device_id_type=MESH)
             for i, (src, dst) in enumerate(((attbuf, att_ref), (qgbuf, qg_ref))):
                 outward[d, g, i] = pltpu.make_async_remote_copy(
-                    src_ref=src.at[d, :, lanes(g)], dst_ref=dst.at[:, columns(head, g)],
+                    src_ref=src.at[d, g], dst_ref=columns(dst, head, g),
                     send_sem=ret_send.at[d - 1, g, i], recv_sem=ret_recv.at[d - 1, g, i],
                     device_id=(seq, other), device_id_type=MESH)
     back = {}
@@ -98,10 +104,10 @@
 
     own = [
         pltpu.make_async_copy(src, dst, local_sem.at[i])
-        for i, (src, dst) in enumerate((
-            (k_ref, kwin.at[block(0)]), (v_ref, vwin.at[block(0)]), (doc_ref, docwin.at[0]),
-            (q_ref.at[:, pl.ds(pl.multiple_of(head * cols, HD), cols)], qbuf.at[0]),
-            (g_ref.at[:, pl.ds(pl.multiple_of(head * cols, HD), cols)], gbuf.at[0])))
+        for i, (src, dst) in enumerate(
+            [(k_ref, kwin.at[block(0)]), (v_ref, vwin.at[block(0)]), (doc_ref, docwin.at[0])]
+            + [(columns(q_ref, head, g), qbuf.at[0, g]) for g in range(groups)]
+            + [(columns(g_ref, head, g), gbuf.at[0, g]) for g in range(groups)])
     ]
     for copy in own:
         copy.start()
@@ -162,8 +168,8 @@
             [jnp.where(near, x[:tok], zero), x[tok:], jnp.where(near, zero, x[:tok])], axis=0)
 
     def tile(d, g):
-        q = qbuf[d, :, lanes(g)]
-        grad = gbuf[d, :, lanes(g)]
+        q = matrix(qbuf, d, g)[...]
+        grad = matrix(gbuf, d, g)[...]
         by_last = (((1,), (1,)), ((), ()))
         s = folded(lax.dot_general(kwin[:, lanes(g)], q, by_last, preferred_element_type=jnp.float32))
         s = s + bias[...]
@@ -175,9 +181,9 @@
         ds = unfolded(p * (dp - delta) * scale).astype(jnp.bfloat16)
         pb = unfolded(p).astype(jnp.bfloat16)
         att = jnp.dot(vt[g], pb, preferred_element_type=jnp.float32)
-        attbuf[d, :, lanes(g)] = jnp.transpose(att).astype(jnp.bfloat16)
+        matrix(attbuf, d, g)[...] = jnp.transpose(att).astype(jnp.bfloat16)
         qg = jnp.dot(kt[g], ds, preferred_element_type=jnp.float32)
-        qgbuf[d, :, lanes(g)] = jnp.transpose(qg).astype(jnp.bfloat16)
+        matrix(qgbuf, d, g)[...] = jnp.transpose(qg).astype(jnp.bfloat16)
         dv = jnp.dot(pb, grad, preferred_element_type=jnp.float32)
         dk = jnp.dot(ds, q, preferred_element_type=jnp.float32)
         if d == 0:
@@ -187,9 +193,8 @@
             vacc[:, lanes(g)] += dv
             kacc[:, lanes(g)] += dk
 
-    mine = pl.ds(pl.multiple_of(head * cols, HD), cols)
-    done = [pltpu.make_async_copy(attbuf.at[0], att_ref.at[:, mine], local_sem.at[0]),
-            pltpu.make_async_copy(qgbuf.at[0], qg_ref.at[:, mine], local_sem.at[1])]
+    done = [pltpu.make_async_copy(src.at[0, g], columns(dst, head, g), local_sem.at[2 * g + i])
+            for g in range(groups) for i, (src, dst) in enumerate(((attbuf, att_ref), (qgbuf, qg_ref)))]
     for g in range(groups):
         for b in steps:
             @pl.when(seq >= b)
@@ -206,9 +211,9 @@
             if d:
                 outward[d, g, 0].start()
                 outward[d, g, 1].start()
-            elif g == groups - 1:
-                for copy in done:
-                    copy.start()
+            else:
+                done[2 * g].start()
+                done[2 * g + 1].start()
         for b in reversed(steps):
             vg_out[b - 1, :, lanes(g)] = vacc[block(b), lanes(g)].astype(jnp.bfloat16)
             kg_out[b - 1, :, lanes(g)] = kacc[block(b), lanes(g)].astype(jnp.bfloat16)
@@ -250,34 +255,51 @@
                 outward[d, g, i].wait_recv()
 
 
+def settle(*refs):
+    sources, places, sem = refs[:4], refs[4:8], refs[8]
+    copies = []
+    for src, dst in zip(sources, places):
+        parts = 4 if len(copies) < 8 else 1
+        size = src.shape[0] // parts
+        for part in range(parts):
+            at = pl.ds(part * size, size)
+            copies.append(pltpu.make_async_copy(src.at[at], dst.at[at], sem.at[len(copies)]))
+    for copy in copies:
+        copy.start()
+    for copy in copies:
+        copy.wait()
+
+
 def on_device(n_seq, n_head, queries, keys, values, out_grad, doc_ids):
     tok, reps, width = queries.shape
     cols = keys.shape[1]
     groups = cols // HD
     rows = tok * reps
     span = (REACH + 1) * tok
+    whole = (tok, reps, width) if reps > 1 else (tok, width)
+    piece = whole[:-1] + (HD,)
     bf16, f32 = jnp.bfloat16, jnp.float32
     dma = pltpu.SemaphoreType.DMA
     anywhere = pl.BlockSpec(memory_space=pl.ANY)
     vmem = pl.BlockSpec(memory_space=pltpu.VMEM)
-    flat = jax.ShapeDtypeStruct((rows, width), bf16)
+    flat = jax.ShapeDtypeStruct(whole, bf16)
     narrow = jax.ShapeDtypeStruct((tok, cols), bf16)
-    att, qg, kg, vg = pl.pallas_call(
+    results = pl.pallas_call(
         functools.partial(kernel, n_seq, n_head, reps),
         out_shape=(flat, flat, narrow, narrow),
         in_specs=[anywhere] * 5,
         out_specs=(anywhere, anywhere, vmem, vmem),
         scratch_shapes=[
-            pltpu.VMEM((n_head, rows, cols), bf16),
-            pltpu.VMEM((n_head, rows, cols), bf16),
+            pltpu.VMEM((n_head, groups) + piece, bf16),
+            pltpu.VMEM((n_head, groups) + piece, bf16),
             pltpu.VMEM((span, cols), bf16),
             pltpu.VMEM((span, cols), bf16),
             pltpu.VMEM((groups, HD, span), bf16),
             pltpu.VMEM((groups, HD, span), bf16),
             pltpu.VMEM((REACH + 1, 1, tok), jnp.int32),
             pltpu.VMEM((REACH * tok, rows), f32),
-            pltpu.VMEM((n_head, rows, cols), bf16),
-            pltpu.VMEM((n_head, rows, cols), bf16),
+            pltpu.VMEM((n_head, groups) + piece, bf16),
+            pltpu.VMEM((n_head, groups) + piece, bf16),
             pltpu.VMEM((span, cols), f32),
             pltpu.VMEM((span, cols), f32),
             pltpu.VMEM((REACH, tok, cols), bf16),
@@ -288,17 +310,26 @@
             dma((n_head - 1, groups, 2)), dma((n_head - 1, groups, 2)),
             dma((n_head - 1, groups, 2)), dma((n_head - 1, groups, 2)),
             dma((REACH, groups, 2)), dma((REACH, groups, 2)),
-            dma((5,)),
+            dma((3 + 2 * groups,)),
         ],
         compiler_params=pltpu.CompilerParams(
-            collective_id=0, has_side_effects=True, vmem_limit_bytes=32 * 2**20),
+            collective_id=0, has_side_effects=True, vmem_limit_bytes=LIMIT),
         cost_estimate=pl.CostEstimate(
             flops=12 * n_head * groups * rows * span * HD,
             bytes_accessed=8 * rows * width + 8 * tok * cols,
             transcendentals=n_head * groups * rows * REACH * tok),
         name="attention_layer",
-    )(queries.reshape(rows, width), keys, values, out_grad.reshape(rows, width), doc_ids.reshape(1, tok))
-    return (att.reshape(tok, reps, width), qg.reshape(tok, reps, width), kg, vg)
+    )(queries.reshape(whole), keys, values, out_grad.reshape(whole), doc_ids.reshape(1, tok))
+    att, qg, kg, vg = pl.pallas_call(
+        settle,
+        out_shape=(flat, flat, narrow, narrow),
+        in_specs=[anywhere] * 4,
+        out_specs=(anywhere,) * 4,
+        scratch_shapes=[dma((10,))],
+        compiler_params=pltpu.CompilerParams(vmem_limit_bytes=LIMIT),
+        name="settle",
+    )(*results)
+    return (att.reshape(queries.shape), qg.reshape(queries.shape), kg, vg)
 
 
 def solution(mesh):

time: 34.9 us -> 67.5 us (1.93)
  Pallas kernels: 28.7 us -> 66.7 us
  local copies, waits for them, and re-layouts: 5.39 us -> 0 us
    pallas_call x0 -> x1, Pallas kernels: none -> 36.9 us  [on_device(): pl.pallas_call(settle, out_shape=(flat, flat, narrow, narrow), in_specs=[...]
    reshape x4 -> x0, local copies, waits for them, and re-layouts: 3.48 us -> none  [the longest x2 1.98 us: on_device(): return (att.reshape(tok, reps, width), qg.reshape(tok, reps, width), kg, vg)]
    unnamed x10 -> x0, local copies, waits for them, and re-layouts: 1.91 us -> none
    pallas_call x1, Pallas kernels: 28.7 us -> 29.7 us  [on_device(): pl.pallas_call(functools.partial(kernel, n_seq, n_head, reps), out_shape=...]
where the time goes in v3:
time: 67.5 us; the launch traced here: 67.3 us
  Pallas kernels  66.7 us (99%)
    pallas_call x1, Pallas kernels, on_device(): pl.pallas_call(settle, out_shape=(flat, flat, narrow, narrow), in_specs=[...  36.9 us
    pallas_call x1, Pallas kernels, on_device(): pl.pallas_call(functools.partial(kernel, n_seq, n_head, reps), out_shape=...  29.7 us

profile of v3, /device:TPU:1, one launch (start us, length us, event | category | flops | bytes accessed | tf_op | source)
XLA Modules:
  0.0 67.3 jit_solution(14324952805262385478)
XLA Ops:
  0.6 29.7 %attention_layer.1 = (bf16[128,2,1024]{2,1,0:T(2,128)(2,1)}, bf16[128,2,1024]{2,1,0:T(2,128)(2,1)}, bf16[128,256]{1,0:T(8,128)(2,1)}, bf16[128,256]{1,0:T(8,128)(2,1)}) custom-call(bf16[128,2,1024]{2,1,0:T(2,128)(2,1)} %q_ref.1, bf16[128,256]{1,0:T(8,128)(2,1)} %k_ref.1, bf16[128,256]{1,0:T(8,128)(2,1)} %v_ref.1, bf16[128,2,1024]{2,1,0:T(2,128)(2,1)} %g_ref.1, ...), custom_call_target="tpu_custom_call" | custom-call | flops 1610612736 | bytes 2359296 | tf_op jit(solution)/shard_map/attention_layer/pallas_call | solution.py:287
  30.4 36.9 %settle.1 = (bf16[128,2,1024]{2,1,0:T(2,128)(2,1)}, bf16[128,2,1024]{2,1,0:T(2,128)(2,1)}, bf16[128,256]{1,0:T(8,128)(2,1)}, bf16[128,256]{1,0:T(8,128)(2,1)}) custom-call(bf16[128,2,1024]{2,1,0:T(2,128)(2,1)} %get-tuple-element.8.refs_0_, bf16[128,2,1024]{2,1,0:T(2,128)(2,1)} %get-tuple-element.9.refs_1_, bf16[128,256]{1,0:T(8,128)(2,1)} %get-tuple-element.10.refs_2_, ...), custom_call_target="tpu_custom_call" | custom-call | tf_op jit(solution)/shard_map/settle/pallas_call | solution.py:323

commit v4 on v3

--- a/solution.py
+++ b/solution.py
@@ -10,7 +10,7 @@
 
 HD = 128
 REACH = 3
-LIMIT = 60 * 2**20
+LIMIT = 32 * 2**20
 MESH = pl.DeviceIdType.MESH
 
 

time: 67.5 us -> 35.2 us (0.52)
  Pallas kernels: 66.7 us -> 29.8 us
  local copies, waits for them, and re-layouts: 0 us -> 4.41 us
    pallas_call x1, Pallas kernels: 36.9 us -> 1.09 us  [on_device(): pl.pallas_call(settle, out_shape=(flat, flat, narrow, narrow), in_specs=[...]
    unnamed x0 -> x10, local copies, waits for them, and re-layouts: none -> 4.41 us
    pallas_call x1, Pallas kernels: 29.7 us -> 28.7 us  [on_device(): pl.pallas_call(functools.partial(kernel, n_seq, n_head, reps), out_shape=...]
where the time goes in v4:
time: 35.2 us; the launch traced here: 34.8 us
  Pallas kernels  29.8 us (85%)
  local copies, waits for them, and re-layouts  4.41 us (13%)
  between operations  0.65 us (2%)
    pallas_call x1, Pallas kernels, on_device(): pl.pallas_call(functools.partial(kernel, n_seq, n_head, reps), out_shape=...  28.7 us
    unnamed x10, local copies, waits for them, and re-layouts  4.41 us
    pallas_call x1, Pallas kernels, on_device(): pl.pallas_call(settle, out_shape=(flat, flat, narrow, narrow), in_specs=[...  1.09 us

profile of v4, /device:TPU:1, one launch (start us, length us, event | category | flops | bytes accessed | tf_op | source)
XLA Modules:
  0.0 34.8 jit_solution(6940042272023237821)
XLA Ops:
  0.6 0.0 copy-start.4
  0.6 0.6 %copy-done.4 = s32[128]{0:T(128)S(1)} copy-done((s32[128]{0:T(128)S(1)}, s32[128]{0:T(128)}, u32[]{:S(2)}) %copy-start.4) | copy-done | bytes 536
  1.3 0.0 copy-start
  1.3 1.0 %copy-done = bf16[128,2,1024]{2,1,0:T(2,128)(2,1)S(1)} copy-done((bf16[128,2,1024]{2,1,0:T(2,128)(2,1)S(1)}, bf16[128,2,1024]{2,1,0:T(2,128)(2,1)}, u32[]{:S(2)}) %copy-start) | copy-done | bytes 524312
  2.3 0.0 copy-start.1
  2.3 1.0 %copy-done.1 = bf16[128,2,1024]{2,1,0:T(2,128)(2,1)S(1)} copy-done((bf16[128,2,1024]{2,1,0:T(2,128)(2,1)S(1)}, bf16[128,2,1024]{2,1,0:T(2,128)(2,1)}, u32[]{:S(2)}) %copy-start.1) | copy-done | bytes 524312
  3.4 0.0 copy-start.2
  3.4 0.8 %copy-done.2 = bf16[128,256]{1,0:T(8,128)(2,1)S(1)} copy-done((bf16[128,256]{1,0:T(8,128)(2,1)S(1)}, bf16[128,256]{1,0:T(8,128)(2,1)}, u32[]{:S(2)}) %copy-start.2) | copy-done | bytes 65560
  4.2 0.0 copy-start.3
  4.2 0.8 %copy-done.3 = bf16[128,256]{1,0:T(8,128)(2,1)S(1)} copy-done((bf16[128,256]{1,0:T(8,128)(2,1)S(1)}, bf16[128,256]{1,0:T(8,128)(2,1)}, u32[]{:S(2)}) %copy-start.3) | copy-done | bytes 65560
  5.1 28.7 %attention_layer.1 = (bf16[128,2,1024]{2,1,0:T(2,128)(2,1)S(1)}, bf16[128,2,1024]{2,1,0:T(2,128)(2,1)S(1)}, bf16[128,256]{1,0:T(8,128)(2,1)S(1)}, bf16[128,256]{1,0:T(8,128)(2,1)S(1)}) custom-call(bf16[128,2,1024]{2,1,0:T(2,128)(2,1)S(1)} %copy-done, bf16[128,256]{1,0:T(8,128)(2,1)S(1)} %copy-done.2, bf16[128,256]{1,0:T(8,128)(2,1)S(1)} %copy-done.3, ...), custom_call_target="tpu_custom_call" | custom-call | flops 1610612736 | bytes 2359296 | tf_op jit(solution)/shard_map/attention_layer/pallas_call | solution.py:287
  33.8 1.1 %settle.1 = (bf16[128,2,1024]{2,1,0:T(2,128)(2,1)}, bf16[128,2,1024]{2,1,0:T(2,128)(2,1)}, bf16[128,256]{1,0:T(8,128)(2,1)}, bf16[128,256]{1,0:T(8,128)(2,1)}) custom-call(bf16[128,2,1024]{2,1,0:T(2,128)(2,1)S(1)} %get-tuple-element.8.refs_0_, bf16[128,2,1024]{2,1,0:T(2,128)(2,1)S(1)} %get-tuple-element.9.refs_1_, ...), custom_call_target="tpu_custom_call" | custom-call | tf_op jit(solution)/shard_map/settle/pallas_call | solution.py:323
Async XLA Ops:
  0.6 0.7 %copy-start.4 = (s32[128]{0:T(128)S(1)}, s32[128]{0:T(128)}, u32[]{:S(2)}) copy-start(s32[128]{0:T(128)} %param.9) | copy-start | bytes 1540
  1.3 1.0 %copy-start = (bf16[128,2,1024]{2,1,0:T(2,128)(2,1)S(1)}, bf16[128,2,1024]{2,1,0:T(2,128)(2,1)}, u32[]{:S(2)}) copy-start(bf16[128,2,1024]{2,1,0:T(2,128)(2,1)} %q_ref.1) | copy-start | bytes 1572868
  2.3 1.0 %copy-start.1 = (bf16[128,2,1024]{2,1,0:T(2,128)(2,1)S(1)}, bf16[128,2,1024]{2,1,0:T(2,128)(2,1)}, u32[]{:S(2)}) copy-start(bf16[128,2,1024]{2,1,0:T(2,128)(2,1)} %g_ref.1) | copy-start | bytes 1572868
  3.4 0.8 %copy-start.2 = (bf16[128,256]{1,0:T(8,128)(2,1)S(1)}, bf16[128,256]{1,0:T(8,128)(2,1)}, u32[]{:S(2)}) copy-start(bf16[128,256]{1,0:T(8,128)(2,1)} %k_ref.1) | copy-start | bytes 196612
  4.2 0.8 %copy-start.3 = (bf16[128,256]{1,0:T(8,128)(2,1)S(1)}, bf16[128,256]{1,0:T(8,128)(2,1)}, u32[]{:S(2)}) copy-start(bf16[128,256]{1,0:T(8,128)(2,1)} %v_ref.1) | copy-start | bytes 196612

commit v5 on v3

--- a/solution.py
+++ b/solution.py
@@ -29,8 +29,8 @@
     q_ref, k_ref, v_ref, g_ref, doc_ref,
     att_ref, qg_ref, kg_ref, vg_ref,
     qbuf, gbuf, kwin, vwin, kt, vt, docwin, bias, attbuf, qgbuf, kacc, vacc,
-    kg_out, vg_out, kg_in, vg_in,
-    halo_send, halo_recv, in_send, in_recv, ret_send, ret_recv, grad_send, grad_recv, local_sem,
+    kg_out, vg_out, kg_in, vg_in, qall, gall,
+    halo_send, halo_recv, in_send, in_recv, ret_send, ret_recv, grad_send, grad_recv, local_sem, own_sem,
 ):
     seq, head = lax.axis_index("seq"), lax.axis_index("head")
     tok, cols = k_ref.shape
@@ -55,10 +55,10 @@
 
     halo = {}
     for b in steps:
-        pairs = [(doc_ref, docwin.at[b])]
+        pairs = [(docwin.at[0], docwin.at[b])]
         for g in range(groups):
-            pairs.append((k_ref.at[:, lanes(g)], kwin.at[block(b), lanes(g)]))
-            pairs.append((v_ref.at[:, lanes(g)], vwin.at[block(b), lanes(g)]))
+            pairs.append((kwin.at[block(0), lanes(g)], kwin.at[block(b), lanes(g)]))
+            pairs.append((vwin.at[block(0), lanes(g)], vwin.at[block(b), lanes(g)]))
         for i, (src, dst) in enumerate(pairs):
             halo[b, i] = pltpu.make_async_remote_copy(
                 src_ref=src, dst_ref=dst, send_sem=halo_send.at[b - 1, i],
@@ -69,7 +69,7 @@
     for d in peers:
         other = partner(head, d)
         for g in range(groups):
-            for i, (src, dst) in enumerate(((q_ref, qbuf), (g_ref, gbuf))):
+            for i, (src, dst) in enumerate(((qall, qbuf), (gall, gbuf))):
                 inward[d, g, i] = pltpu.make_async_remote_copy(
                     src_ref=columns(src, other, g), dst_ref=dst.at[d, g],
                     send_sem=in_send.at[d - 1, g, i], recv_sem=in_recv.at[d - 1, g, i],
@@ -104,12 +104,19 @@
 
     own = [
         pltpu.make_async_copy(src, dst, local_sem.at[i])
-        for i, (src, dst) in enumerate(
-            [(k_ref, kwin.at[block(0)]), (v_ref, vwin.at[block(0)]), (doc_ref, docwin.at[0])]
-            + [(columns(q_ref, head, g), qbuf.at[0, g]) for g in range(groups)]
-            + [(columns(g_ref, head, g), gbuf.at[0, g]) for g in range(groups)])
+        for i, (src, dst) in enumerate((
+            (doc_ref, docwin.at[0]), (k_ref, kwin.at[block(0)]), (v_ref, vwin.at[block(0)]),
+            (q_ref, qall), (g_ref, gall)))
+    ]
+    mine = [
+        pltpu.make_async_copy(columns(src, head, g), dst.at[0, g], own_sem.at[g, i])
+        for g in range(groups) for i, (src, dst) in enumerate(((qall, qbuf), (gall, gbuf)))
     ]
     for copy in own:
+        copy.start()
+    for copy in own:
+        copy.wait()
+    for copy in mine:
         copy.start()
     pl.semaphore_wait(barrier, count)
 
@@ -133,7 +140,7 @@
     key_of = lax.broadcasted_iota(jnp.int32, (tok, rows), 0)
     token_of = lax.broadcasted_iota(jnp.int32, (tok, rows), 1) // reps
     near = key_of <= token_of
-    for copy in own:
+    for copy in mine:
         copy.wait()
     for b in steps:
         @pl.when(seq >= b)
@@ -193,7 +200,7 @@
             vacc[:, lanes(g)] += dv
             kacc[:, lanes(g)] += dk
 
-    done = [pltpu.make_async_copy(src.at[0, g], columns(dst, head, g), local_sem.at[2 * g + i])
+    done = [pltpu.make_async_copy(src.at[0, g], columns(dst, head, g), own_sem.at[g, i])
             for g in range(groups) for i, (src, dst) in enumerate(((attbuf, att_ref), (qgbuf, qg_ref)))]
     for g in range(groups):
         for b in steps:
@@ -256,18 +263,22 @@
 
 
 def settle(*refs):
-    sources, places, sem = refs[:4], refs[4:8], refs[8]
+    sources, places, held, sem = refs[:4], refs[4:8], refs[8:12], refs[12]
     copies = []
-    for src, dst in zip(sources, places):
-        parts = 4 if len(copies) < 8 else 1
+    for src, dst, mid in zip(sources, places, held):
+        parts = 2
         size = src.shape[0] // parts
         for part in range(parts):
             at = pl.ds(part * size, size)
-            copies.append(pltpu.make_async_copy(src.at[at], dst.at[at], sem.at[len(copies)]))
-    for copy in copies:
-        copy.start()
-    for copy in copies:
-        copy.wait()
+            copies.append((pltpu.make_async_copy(src.at[at], mid.at[at], sem.at[0, len(copies)]),
+                           pltpu.make_async_copy(mid.at[at], dst.at[at], sem.at[1, len(copies)])))
+    for into, _ in copies:
+        into.start()
+    for into, out in copies:
+        into.wait()
+        out.start()
+    for _, out in copies:
+        out.wait()
 
 
 def on_device(n_seq, n_head, queries, keys, values, out_grad, doc_ids):
@@ -306,11 +317,13 @@
             pltpu.VMEM((REACH, tok, cols), bf16),
             pltpu.VMEM((REACH, tok, cols), bf16),
             pltpu.VMEM((REACH, tok, cols), bf16),
+            pltpu.VMEM(whole, bf16),
+            pltpu.VMEM(whole, bf16),
             dma((REACH, 1 + 2 * groups)), dma((REACH, 1 + 2 * groups)),
             dma((n_head - 1, groups, 2)), dma((n_head - 1, groups, 2)),
             dma((n_head - 1, groups, 2)), dma((n_head - 1, groups, 2)),
             dma((REACH, groups, 2)), dma((REACH, groups, 2)),
-            dma((3 + 2 * groups,)),
+            dma((5,)), dma((groups, 2)),
         ],
         compiler_params=pltpu.CompilerParams(
             collective_id=0, has_side_effects=True, vmem_limit_bytes=LIMIT),
@@ -325,7 +338,7 @@
         out_shape=(flat, flat, narrow, narrow),
         in_specs=[anywhere] * 4,
         out_specs=(anywhere,) * 4,
-        scratch_shapes=[dma((10,))],
+        scratch_shapes=[pltpu.VMEM(x.shape, x.dtype) for x in results] + [dma((2, 8))],
         compiler_params=pltpu.CompilerParams(vmem_limit_bytes=LIMIT),
         name="settle",
     )(*results)

time: 67.5 us -> 32.4 us (0.48)
  Pallas kernels: 66.7 us -> 31.6 us
    pallas_call x1, Pallas kernels: 36.9 us -> 2.08 us  [on_device(): pl.pallas_call(settle, out_shape=(flat, flat, narrow, narrow), in_specs=[...]
where the time goes in v5:
time: 32.4 us; the launch traced here: 32.3 us
  Pallas kernels  31.6 us (98%)
  between operations  0.64 us (2%)
    pallas_call x1, Pallas kernels, on_device(): pl.pallas_call(functools.partial(kernel, n_seq, n_head, reps), out_shape=...  29.5 us
    pallas_call x1, Pallas kernels, on_device(): pl.pallas_call(settle, out_shape=(flat, flat, narrow, narrow), in_specs=[...  2.08 us

profile of v5, /device:TPU:1, one launch (start us, length us, event | category | flops | bytes accessed | tf_op | source)
XLA Modules:
  0.0 32.3 jit_solution(492060776452066586)
XLA Ops:
  0.6 29.5 %attention_layer.1 = (bf16[128,2,1024]{2,1,0:T(2,128)(2,1)}, bf16[128,2,1024]{2,1,0:T(2,128)(2,1)}, bf16[128,256]{1,0:T(8,128)(2,1)}, bf16[128,256]{1,0:T(8,128)(2,1)}) custom-call(bf16[128,2,1024]{2,1,0:T(2,128)(2,1)} %q_ref.1, bf16[128,256]{1,0:T(8,128)(2,1)} %k_ref.1, bf16[128,256]{1,0:T(8,128)(2,1)} %v_ref.1, bf16[128,2,1024]{2,1,0:T(2,128)(2,1)} %g_ref.1, ...), custom_call_target="tpu_custom_call" | custom-call | flops 1610612736 | bytes 2359296 | tf_op jit(solution)/shard_map/attention_layer/pallas_call | solution.py:298
  30.2 2.1 %settle.1 = (bf16[128,2,1024]{2,1,0:T(2,128)(2,1)}, bf16[128,2,1024]{2,1,0:T(2,128)(2,1)}, bf16[128,256]{1,0:T(8,128)(2,1)}, bf16[128,256]{1,0:T(8,128)(2,1)}) custom-call(bf16[128,2,1024]{2,1,0:T(2,128)(2,1)} %get-tuple-element.8.refs_0_, bf16[128,2,1024]{2,1,0:T(2,128)(2,1)} %get-tuple-element.9.refs_1_, bf16[128,256]{1,0:T(8,128)(2,1)} %get-tuple-element.10.refs_2_, ...), custom_call_target="tpu_custom_call" | custom-call | tf_op jit(solution)/shard_map/settle/pallas_call | solution.py:336

commit v6 on v5

--- a/solution.py
+++ b/solution.py
@@ -120,15 +120,18 @@
         copy.start()
     pl.semaphore_wait(barrier, count)
 
+    far = [d for d in peers if d > 1]
     for g in range(groups):
+        for d in far:
+            for i in range(2):
+                inward[d, g, i].start()
         for b in reversed(steps):
             @pl.when(seq + b < n_seq)
             def _():
                 for i in ((0, 1, 2) if g == 0 else (1 + 2 * g, 2 + 2 * g)):
                     halo[b, i].start()
-        for d in reversed(peers):
-            for i in range(2):
-                inward[d, g, i].start()
+        for i in range(2):
+            inward[1, g, i].start()
 
     for b in steps:
         @pl.when(seq < b)
@@ -202,6 +205,7 @@
 
     done = [pltpu.make_async_copy(src.at[0, g], columns(dst, head, g), own_sem.at[g, i])
             for g in range(groups) for i, (src, dst) in enumerate(((attbuf, att_ref), (qgbuf, qg_ref)))]
+    held_back = []
     for g in range(groups):
         for b in steps:
             @pl.when(seq >= b)
@@ -211,11 +215,18 @@
         kt[g] = jnp.transpose(kwin[:, lanes(g)])
         vt[g] = jnp.transpose(vwin[:, lanes(g)])
         for d in range(n_head):
+            if d == 2 and g == groups - 1:
+                for copy in (inward[e, h, i] for e in far for h in range(groups) for i in range(2)):
+                    copy.wait_send()
+                for copy in held_back:
+                    copy.start()
             if d:
                 inward[d, g, 0].wait_recv()
                 inward[d, g, 1].wait_recv()
             tile(d, g)
-            if d:
+            if d in far and g < groups - 1:
+                held_back += [outward[d, g, 0], outward[d, g, 1]]
+            elif d:
                 outward[d, g, 0].start()
                 outward[d, g, 1].start()
             else:
@@ -257,7 +268,8 @@
     for d in peers:
         for g in range(groups):
             for i in range(2):
-                inward[d, g, i].wait_send()
+                if d not in far:
+                    inward[d, g, i].wait_send()
                 outward[d, g, i].wait_send()
                 outward[d, g, i].wait_recv()
 

time: 32.4 us -> 35.1 us (1.083)
  the two profiles are of different devices: /device:TPU:1 before, /device:TPU:17 now
where the time goes in v6:
time: 35.1 us; the launch traced here: 35 us
  Pallas kernels  34.3 us (98%)
  between operations  0.64 us (2%)
    pallas_call x1, Pallas kernels, on_device(): pl.pallas_call(functools.partial(kernel, n_seq, n_head, reps), out_shape=...  32.3 us
    pallas_call x1, Pallas kernels, on_device(): pl.pallas_call(settle, out_shape=(flat, flat, narrow, narrow), in_specs=[...  2.08 us

profile of v6, /device:TPU:17, one launch (start us, length us, event | category | flops | bytes accessed | tf_op | source)
XLA Modules:
  0.0 35.0 jit_solution(5007538723619560570)
XLA Ops:
  0.6 32.3 %attention_layer.1 = (bf16[128,2,1024]{2,1,0:T(2,128)(2,1)}, bf16[128,2,1024]{2,1,0:T(2,128)(2,1)}, bf16[128,256]{1,0:T(8,128)(2,1)}, bf16[128,256]{1,0:T(8,128)(2,1)}) custom-call(bf16[128,2,1024]{2,1,0:T(2,128)(2,1)} %q_ref.1, bf16[128,256]{1,0:T(8,128)(2,1)} %k_ref.1, bf16[128,256]{1,0:T(8,128)(2,1)} %v_ref.1, bf16[128,2,1024]{2,1,0:T(2,128)(2,1)} %g_ref.1, ...), custom_call_target="tpu_custom_call" | custom-call | flops 1610612736 | bytes 2359296 | tf_op jit(solution)/shard_map/attention_layer/pallas_call | solution.py:310
  32.9 2.1 %settle.1 = (bf16[128,2,1024]{2,1,0:T(2,128)(2,1)}, bf16[128,2,1024]{2,1,0:T(2,128)(2,1)}, bf16[128,256]{1,0:T(8,128)(2,1)}, bf16[128,256]{1,0:T(8,128)(2,1)}) custom-call(bf16[128,2,1024]{2,1,0:T(2,128)(2,1)} %get-tuple-element.8.refs_0_, bf16[128,2,1024]{2,1,0:T(2,128)(2,1)} %get-tuple-element.9.refs_1_, bf16[128,256]{1,0:T(8,128)(2,1)} %get-tuple-element.10.refs_2_, ...), custom_call_target="tpu_custom_call" | custom-call | tf_op jit(solution)/shard_map/settle/pallas_call | solution.py:348

commit v7 on v5

--- a/solution.py
+++ b/solution.py
@@ -120,15 +120,18 @@
         copy.start()
     pl.semaphore_wait(barrier, count)
 
+    for d in peers[1:]:
+        inward[d, 0, 0].start()
+        inward[d, 0, 1].start()
     for g in range(groups):
         for b in reversed(steps):
             @pl.when(seq + b < n_seq)
             def _():
                 for i in ((0, 1, 2) if g == 0 else (1 + 2 * g, 2 + 2 * g)):
                     halo[b, i].start()
-        for d in reversed(peers):
-            for i in range(2):
-                inward[d, g, i].start()
+        for d in (peers if g else peers[:1]):
+            inward[d, g, 0].start()
+            inward[d, g, 1].start()
 
     for b in steps:
         @pl.when(seq < b)
@@ -266,7 +269,7 @@
     sources, places, held, sem = refs[:4], refs[4:8], refs[8:12], refs[12]
     copies = []
     for src, dst, mid in zip(sources, places, held):
-        parts = 2
+        parts = 4 if len(copies) < 8 else 1
         size = src.shape[0] // parts
         for part in range(parts):
             at = pl.ds(part * size, size)
@@ -338,7 +341,7 @@
         out_shape=(flat, flat, narrow, narrow),
         in_specs=[anywhere] * 4,
         out_specs=(anywhere,) * 4,
-        scratch_shapes=[pltpu.VMEM(x.shape, x.dtype) for x in results] + [dma((2, 8))],
+        scratch_shapes=[pltpu.VMEM(x.shape, x.dtype) for x in results] + [dma((2, 10))],
         compiler_params=pltpu.CompilerParams(vmem_limit_bytes=LIMIT),
         name="settle",
     )(*results)

time: 32.4 us -> 32.5 us (level)
  no operation moved by 1% of the time
where the time goes in v7:
time: 32.5 us; the launch traced here: 32.3 us
  Pallas kernels  31.7 us (98%)
  between operations  0.64 us (2%)
    pallas_call x1, Pallas kernels, on_device(): pl.pallas_call(functools.partial(kernel, n_seq, n_head, reps), out_shape=...  29.5 us
    pallas_call x1, Pallas kernels, on_device(): pl.pallas_call(settle, out_shape=(flat, flat, narrow, narrow), in_specs=[...  2.16 us

profile of v7, /device:TPU:1, one launch (start us, length us, event | category | flops | bytes accessed | tf_op | source)
XLA Modules:
  0.0 32.3 jit_solution(18354190150886599074)
XLA Ops:
  0.6 29.5 %attention_layer.1 = (bf16[128,2,1024]{2,1,0:T(2,128)(2,1)}, bf16[128,2,1024]{2,1,0:T(2,128)(2,1)}, bf16[128,256]{1,0:T(8,128)(2,1)}, bf16[128,256]{1,0:T(8,128)(2,1)}) custom-call(bf16[128,2,1024]{2,1,0:T(2,128)(2,1)} %q_ref.1, bf16[128,256]{1,0:T(8,128)(2,1)} %k_ref.1, bf16[128,256]{1,0:T(8,128)(2,1)} %v_ref.1, bf16[128,2,1024]{2,1,0:T(2,128)(2,1)} %g_ref.1, ...), custom_call_target="tpu_custom_call" | custom-call | flops 1610612736 | bytes 2359296 | tf_op jit(solution)/shard_map/attention_layer/pallas_call | solution.py:301
  30.2 2.2 %settle.1 = (bf16[128,2,1024]{2,1,0:T(2,128)(2,1)}, bf16[128,2,1024]{2,1,0:T(2,128)(2,1)}, bf16[128,256]{1,0:T(8,128)(2,1)}, bf16[128,256]{1,0:T(8,128)(2,1)}) custom-call(bf16[128,2,1024]{2,1,0:T(2,128)(2,1)} %get-tuple-element.8.refs_0_, bf16[128,2,1024]{2,1,0:T(2,128)(2,1)} %get-tuple-element.9.refs_1_, bf16[128,256]{1,0:T(8,128)(2,1)} %get-tuple-element.10.refs_2_, ...), custom_call_target="tpu_custom_call" | custom-call | tf_op jit(solution)/shard_map/settle/pallas_call | solution.py:339
